TPU v7x, 128 devices: a whole 4x4x4 slice. The times are simulated.
128 devices in a mesh: seq: 16 (over y, x), grp: 8 (over z, core).
Axes of the slice: x: 4, y: 4, z: 4, core: 2. Of those that a mesh axis runs over, the one named last changes fastest.
Arguments:
- tokens: bfloat16 [2, 4096, 2048], P(None, 'seq'), may hold values from -6 to 6
- lengths: int32 [2], replicated, may hold values from 2048 to 4096, as said below
- norm_attn: float32 [2048], replicated, may hold values from 0.5 to 1.5
- w_query: bfloat16 [2048, 2048], P(None, 'grp'), may hold values from -0.125 to 0.125
- w_key: bfloat16 [2048, 1024], P(None, 'grp'), may hold values from -0.125 to 0.125
- w_value: bfloat16 [2048, 1024], P(None, 'grp'), may hold values from -0.125 to 0.125
- w_gate: bfloat16 [2048, 16], P(None, 'grp'), may hold values from -0.125 to 0.125
- norm_query: float32 [128], replicated, may hold values from 1 to 1.6
- norm_key: float32 [128], replicated, may hold values from 1 to 1.6
- w_out: bfloat16 [2048, 2048], P('grp'), may hold values from -2 to 2
- norm_ffn: float32 [2048], replicated, may hold values from 0.5 to 1.5
- w_ffn_gate: bfloat16 [2048, 6144], P(None, 'grp'), may hold values from -0.125 to 0.125
- w_ffn_up: bfloat16 [2048, 6144], P(None, 'grp'), may hold values from -0.125 to 0.125
- w_down: bfloat16 [6144, 2048], P('grp'), may hold values from -0.109375 to 0.109375
- cotangent: bfloat16 [2, 4096, 2048], P(None, 'seq'), may hold values from -6 to 6
Outputs:
- mixed: bfloat16 [2, 4096, 2048], P(None, 'seq')
- grad_tokens: bfloat16 [2, 4096, 2048], P(None, 'seq')
- grad_norm_attn: float32 [2048], replicated
- grad_w_query: float32 [2048, 2048], P(None, 'grp')
- grad_w_key: float32 [2048, 1024], P(None, 'grp')
- grad_w_value: float32 [2048, 1024], P(None, 'grp')
- grad_w_gate: float32 [2048, 16], P(None, 'grp')
- grad_norm_query: float32 [128], replicated
- grad_norm_key: float32 [128], replicated
- grad_w_out: float32 [2048, 2048], P('grp')
- grad_norm_ffn: float32 [2048], replicated
- grad_w_ffn_gate: float32 [2048, 6144], P(None, 'grp')
- grad_w_ffn_up: float32 [2048, 6144], P(None, 'grp')
- grad_w_down: float32 [6144, 2048], P('grp')
Inputs may be any that keep to these rules, and one draw needn't show every extreme that they name: Bucket b holds one sequence of lengths[b] true tokens at its start, padding after it; exactly one bucket, drawn from the seed, is full with 4096 tokens.
All inputs are finite; a program needn't handle non-finite values.
Results may differ from a plain program's by a relative error of at most 0.025.
Values may be sent and summed in bfloat16 or wider, within the bound.
A program may use at most 192 MiB of HBM per device.

v0:
```python
import functools

import jax
import jax.numpy as jnp
from jax import lax
from jax.sharding import Mesh
from jax.sharding import PartitionSpec as P

GRP = ("grp_0", "grp_1")
SEQ = ("seq_0", "seq_1")
SEQ_GRP = ("seq_0", "seq_1", "grp_0", "grp_1")


epsilon = 1e-06
rope_base = 1000000.0


def in_blocks(value, dim, count):
    lengths = value.shape
    pieces = value.reshape(*lengths[:dim], count, lengths[dim] // count, *lengths[dim + 1 :])
    return jnp.moveaxis(pieces, dim, 0)


def sent_and_summed(value, axis, dim):
    count = lax.axis_size(axis)
    pieces = lax.all_to_all(in_blocks(value, dim, count), axis, 0, 0, tiled=True)
    return jnp.sum(pieces.astype(jnp.float32), axis=0)


def sent_to_all(value, axis):
    copies = jnp.broadcast_to(value, (lax.axis_size(axis), *value.shape))
    return lax.all_to_all(copies, axis, split_axis=0, concat_axis=0, tiled=True)


def joined_along(pieces, dim):
    lengths = list(pieces.shape[1:])
    lengths[dim] *= pieces.shape[0]
    return jnp.moveaxis(pieces, 0, dim).reshape(lengths)


def collect(value, axis, dim):
    pieces = sent_to_all(value, axis)
    return joined_along(pieces, dim)


def sent_together(arrays, axis, dim, along):
    ends, at = ([], 0)
    for a in arrays[:-1]:
        at += a.shape[along]
        ends.append(at)
    both = jnp.concatenate(arrays, axis=along)
    return tuple(jnp.split(lax.all_gather(both, axis, axis=dim, tiled=True), ends, axis=along))


def sent_together_2(arrays, axis, dim, along):
    both = jnp.concatenate(arrays, axis=along)
    whole, at, done = (lax.psum_scatter(both, axis, scatter_dimension=dim, tiled=True), 0, [])
    for a in arrays:
        done.append(lax.slice_in_dim(whole, at, at + a.shape[along], axis=along))
        at += a.shape[along]
    return tuple(done)


def by_axis(value, axes):
    return functools.reduce(lax.psum, axes, value)


def unit_scale(values):
    inverse = lax.rsqrt(jnp.mean(values * values, axis=-1, keepdims=True) + epsilon)
    return (values * inverse, inverse)


def norm_back(grad_unit, unit, inverse):
    return inverse * (grad_unit - unit * jnp.mean(grad_unit * unit, axis=-1, keepdims=True))


def rotate(values, positions, sign):
    half = values.shape[-1] // 2
    freq = rope_base ** (-jnp.arange(half, dtype=jnp.float32) * (2.0 / values.shape[-1]))
    angle = positions.astype(jnp.float32)[:, None] * freq[None, :]
    cosine = jnp.cos(angle)[:, None, :]
    sine = sign * jnp.sin(angle)[:, None, :]
    first = values[..., :half]
    second = values[..., half:]
    return jnp.concatenate(
        [first * cosine - second * sine, second * cosine + first * sine], axis=-1
    )


def row_share(values):
    return sent_and_summed(values.astype(jnp.bfloat16), GRP, 0)


def row_join(values):
    return collect(values, GRP, 0)


def local(
    tokens,
    lengths,
    norm_attn,
    w_query,
    w_key,
    w_value,
    w_gate,
    norm_query,
    norm_key,
    w_out,
    norm_ffn,
    w_ffn_gate,
    w_ffn_up,
    w_down,
    cotangent,
):
    f32 = jnp.float32
    bf16 = jnp.bfloat16
    buckets, per_device, model_width = tokens.shape
    head_count = w_gate.shape[1]
    head_size = norm_query.shape[0]
    kv_count = w_key.shape[1] // head_size
    group_size = head_count // kv_count
    total_rows = buckets * per_device
    full_len = per_device * lax.axis_size(SEQ)
    positions = lax.axis_index(SEQ) * per_device + jnp.arange(per_device, dtype=jnp.int32)
    columns = jnp.arange(full_len, dtype=jnp.int32)
    score_scale = head_size ** (-0.5)
    share_rows = total_rows // lax.axis_size(GRP)
    share_start = lax.axis_index(GRP) * share_rows

    def take_share(values):
        return lax.dynamic_slice_in_dim(values, share_start, share_rows, 0)

    inputs = tokens.astype(f32).reshape(total_rows, model_width)
    unit_one, inverse_one = unit_scale(inputs)
    normed = (unit_one * norm_attn).astype(bf16)
    query_raw = jnp.dot(normed, w_query, preferred_element_type=f32).reshape(
        buckets, per_device, head_count, head_size
    )
    key_raw = jnp.dot(normed, w_key, preferred_element_type=f32).reshape(
        buckets, per_device, kv_count, head_size
    )
    value_low = (
        jnp.dot(normed, w_value, preferred_element_type=f32)
        .astype(bf16)
        .reshape(buckets, per_device, kv_count, head_size)
    )
    logits = jnp.dot(normed, w_gate, preferred_element_type=f32).reshape(
        buckets, per_device, head_count
    )
    query_unit, query_inverse = unit_scale(query_raw)
    key_unit, key_inverse = unit_scale(key_raw)
    query_low = (
        rotate(query_unit * norm_query, positions, 1.0)
        .astype(bf16)
        .reshape(buckets, per_device, kv_count, group_size, head_size)
    )
    key_low = rotate(key_unit * norm_key, positions, 1.0).astype(bf16)
    keys_all, values_all = sent_together((key_low, value_low), SEQ, 1, 0)
    allowed = (columns[None, None, :] <= positions[None, :, None]) & (
        columns[None, None, :] < lengths[:, None, None]
    )
    allowed = allowed[:, None, None, :, :]
    scores = (
        jnp.einsum("bqkgd,blkd->bkgql", query_low, keys_all, preferred_element_type=f32)
        * score_scale
    )
    scores = jnp.where(allowed, scores, -1e30)
    highest = jnp.max(scores, axis=-1, keepdims=True)
    summed = jnp.sum(jnp.exp(scores - highest), axis=-1, keepdims=True)
    log_total = highest + jnp.log(summed)
    probs_low = jnp.exp(scores - log_total).astype(bf16)
    attended = jnp.einsum(
        "bkgql,blkd->bqkgd", probs_low, values_all, preferred_element_type=f32
    ).reshape(buckets, per_device, head_count, head_size)
    gate_prob = jax.nn.sigmoid(logits)
    gated = (
        (attended * gate_prob[..., None]).astype(bf16).reshape(total_rows, head_count * head_size)
    )
    attn_part = jnp.dot(gated, w_out, preferred_element_type=f32)
    middle = take_share(inputs) + row_share(attn_part)
    unit_two, inverse_two = unit_scale(middle)
    normed_two = row_join((unit_two * norm_ffn).astype(bf16))
    gate_pre = jnp.dot(normed_two, w_ffn_gate, preferred_element_type=f32)
    up_proj = jnp.dot(normed_two, w_ffn_up, preferred_element_type=f32)
    gate_sig = jax.nn.sigmoid(gate_pre)
    hidden = (gate_pre * gate_sig * up_proj).astype(bf16)
    feed_part = jnp.dot(hidden, w_down, preferred_element_type=f32)
    mixed = row_join((middle + row_share(feed_part)).astype(bf16))
    mixed = mixed.reshape(buckets, per_device, model_width)
    live_rows = (positions[None, :] < lengths[:, None]).astype(f32)
    loss_ratio = buckets * full_len / jnp.sum(lengths).astype(f32)
    grad_out = (cotangent.astype(f32) * live_rows[:, :, None] * loss_ratio).reshape(
        total_rows, model_width
    )
    grad_out_low = grad_out.astype(bf16)
    grad_down = jnp.dot(hidden.T, grad_out_low, preferred_element_type=f32)
    grad_hidden = jnp.dot(grad_out_low, w_down.T, preferred_element_type=f32)
    grad_gate_pre = (grad_hidden * up_proj * gate_sig * (1.0 + gate_pre * (1.0 - gate_sig))).astype(
        bf16
    )
    grad_up = (grad_hidden * gate_pre * gate_sig).astype(bf16)
    grad_ffn_gate = jnp.dot(normed_two.T, grad_gate_pre, preferred_element_type=f32)
    grad_ffn_up = jnp.dot(normed_two.T, grad_up, preferred_element_type=f32)
    back_two_part = jnp.dot(grad_gate_pre, w_ffn_gate.T, preferred_element_type=f32) + jnp.dot(
        grad_up, w_ffn_up.T, preferred_element_type=f32
    )
    back_two = row_share(back_two_part)
    ffn_gain_rows = back_two * unit_two
    grad_middle = take_share(grad_out) + norm_back(back_two * norm_ffn, unit_two, inverse_two)
    grad_attn_low = row_join(grad_middle.astype(bf16))
    ffn_gain_part = jnp.sum(ffn_gain_rows, axis=0)
    grad_w_out = jnp.dot(gated.T, grad_attn_low, preferred_element_type=f32)
    grad_gated = jnp.dot(grad_attn_low, w_out.T, preferred_element_type=f32).reshape(
        buckets, per_device, head_count, head_size
    )
    grad_logits = (
        (jnp.sum(grad_gated * attended, axis=-1) * gate_prob * (1.0 - gate_prob))
        .astype(bf16)
        .reshape(total_rows, head_count)
    )
    grad_attended = (
        (grad_gated * gate_prob[..., None])
        .astype(bf16)
        .reshape(buckets, per_device, kv_count, group_size, head_size)
    )
    again = (
        jnp.einsum("bqkgd,blkd->bkgql", query_low, keys_all, preferred_element_type=f32)
        * score_scale
    )
    again = jnp.where(allowed, again, -1e30)
    probs = jnp.exp(again - log_total)
    grad_probs = jnp.einsum(
        "bqkgd,blkd->bkgql", grad_attended, values_all, preferred_element_type=f32
    )
    inner_sum = jnp.sum(probs * grad_probs, axis=-1, keepdims=True)
    grad_scores = (probs * (grad_probs - inner_sum)).astype(bf16)
    grad_query_rot = (
        jnp.einsum("bkgql,blkd->bqkgd", grad_scores, keys_all, preferred_element_type=f32)
        * score_scale
    ).reshape(buckets, per_device, head_count, head_size)
    grad_keys_all = (
        jnp.einsum("bkgql,bqkgd->blkd", grad_scores, query_low, preferred_element_type=f32)
        * score_scale
    )
    grad_values_all = jnp.einsum(
        "bkgql,bqkgd->blkd", probs.astype(bf16), grad_attended, preferred_element_type=f32
    )
    grad_key_rot, grad_value = tuple(
        (
            part.astype(jnp.float32)
            for part in sent_together_2(
                (grad_keys_all.astype(jnp.bfloat16), grad_values_all.astype(jnp.bfloat16)),
                SEQ,
                1,
                0,
            )
        )
    )
    grad_value_low = grad_value.astype(bf16).reshape(total_rows, kv_count * head_size)
    query_back = rotate(grad_query_rot, positions, -1.0)
    key_back = rotate(grad_key_rot, positions, -1.0)
    query_gain_part = jnp.sum(query_back * query_unit, axis=(0, 1, 2))
    key_gain_part = jnp.sum(key_back * key_unit, axis=(0, 1, 2))
    grad_query_low = (
        norm_back(query_back * norm_query, query_unit, query_inverse)
        .astype(bf16)
        .reshape(total_rows, head_count * head_size)
    )
    grad_key_low = (
        norm_back(key_back * norm_key, key_unit, key_inverse)
        .astype(bf16)
        .reshape(total_rows, kv_count * head_size)
    )
    grad_w_query = jnp.dot(normed.T, grad_query_low, preferred_element_type=f32)
    grad_w_key = jnp.dot(normed.T, grad_key_low, preferred_element_type=f32)
    grad_w_value = jnp.dot(normed.T, grad_value_low, preferred_element_type=f32)
    grad_w_gate = jnp.dot(normed.T, grad_logits, preferred_element_type=f32)
    back_one_part = jnp.dot(grad_query_low, w_query.T, preferred_element_type=f32) + jnp.dot(
        grad_key_low, w_key.T, preferred_element_type=f32
    )
    back_one_part = (
        back_one_part
        + jnp.dot(grad_value_low, w_value.T, preferred_element_type=f32)
        + jnp.dot(grad_logits, w_gate.T, preferred_element_type=f32)
    )
    back_one = row_share(back_one_part)
    unit_rows = take_share(unit_one)
    attn_gain_part = jnp.sum(back_one * unit_rows, axis=0)
    grad_tokens = row_join(
        (grad_middle + norm_back(back_one * norm_attn, unit_rows, take_share(inverse_one))).astype(
            bf16
        )
    )
    grad_tokens = grad_tokens.reshape(buckets, per_device, model_width)
    grad_norm_query, grad_norm_key, grad_norm_ffn, grad_norm_attn = (
        by_axis(query_gain_part, SEQ_GRP),
        by_axis(key_gain_part, SEQ_GRP),
        by_axis(ffn_gain_part, SEQ_GRP),
        by_axis(attn_gain_part, SEQ_GRP),
    )
    everything = (
        lax.psum(grad_w_query.astype(jnp.bfloat16), SEQ).astype(jnp.float32),
        lax.psum(grad_w_key.astype(jnp.bfloat16), SEQ).astype(jnp.float32),
        lax.psum(grad_w_value.astype(jnp.bfloat16), SEQ).astype(jnp.float32),
        lax.psum(grad_w_gate.astype(jnp.bfloat16), SEQ).astype(jnp.float32),
        lax.psum(grad_w_out.astype(jnp.bfloat16), SEQ).astype(jnp.float32),
        lax.psum(grad_ffn_gate.astype(jnp.bfloat16), SEQ).astype(jnp.float32),
        lax.psum(grad_ffn_up.astype(jnp.bfloat16), SEQ).astype(jnp.float32),
        lax.psum(grad_down.astype(jnp.bfloat16), SEQ).astype(jnp.float32),
    )
    attn_sums = everything[:5]
    ffn_sums = everything[5:]
    return (
        mixed,
        grad_tokens,
        grad_norm_attn,
        attn_sums[0],
        attn_sums[1],
        attn_sums[2],
        attn_sums[3],
        grad_norm_query,
        grad_norm_key,
        attn_sums[4],
        grad_norm_ffn,
        ffn_sums[0],
        ffn_sums[1],
        ffn_sums[2],
    )


def solution(mesh):
    finer = Mesh(mesh.devices.reshape(4, 4, 4, 2), ("seq_0", "seq_1", "grp_0", "grp_1"))
    return jax.shard_map(
        local,
        mesh=finer,
        in_specs=(
            P(None, SEQ, None),
            P(),
            P(),
            P(None, GRP),
            P(None, GRP),
            P(None, GRP),
            P(None, GRP),
            P(),
            P(),
            P(GRP, None),
            P(),
            P(None, GRP),
            P(None, GRP),
            P(GRP, None),
            P(None, SEQ, None),
        ),
        out_specs=(
            P(None, SEQ, None),
            P(None, SEQ, None),
            P(),
            P(None, GRP),
            P(None, GRP),
            P(None, GRP),
            P(None, GRP),
            P(),
            P(),
            P(GRP, None),
            P(),
            P(None, GRP),
            P(None, GRP),
            P(GRP, None),
        ),
        check_vma=False,
    )
```

profile of v0, /device:TPU:1, one launch (start us, length us, event | category | flops | bytes accessed | tf_op | source)
XLA Modules:
  0.0 625.6 jit_solution(4915857613425207393)
XLA Ops:
  41.2 37.5 %all-gather.2.cloned.1.call-done = bf16[4,4096,1,128]{3,1,0,2:T(8,128)(2,1)} async-done(((bf16[4,256,1,128]{3,1,0,2:T(8,128)(2,1)}), bf16[4,4096,1,128]{3,1,0,2:T(8,128)(2,1)}) %all-gather.2.cloned.1.call-update) | async-done | bytes 4194320 | tf_op jit(solution)/shard_map/all_gather | solution.py:52
  88.8 11.4 %multiply_convert_fusion.5 = (bf16[2,256,1,2,128]{1,4,3,0,2:T(8,128)(2,1)}, f32[2,128,2,256]{3,1,2,0:T(8,128)}) fusion(f32[2,256,2]{1,2,0:T(2,128)S(1)} %fusion.23, f32[2,4096,256,2]{2,1,3,0:T(8,128)} %copy-done.2, f32[2,2,256]{2,1,0:T(2,128)S(1)} %log_add_fusion, pred[2,256,4096]{1,2,0:T(8,128)(4,1)S(1)} %copy-done.7, ...), kind=kOutput, calls=%fused_computation.72 | convolution fusion | flops 1090781184 | bytes 21766144 | tf_op jit(solution)/shard_map/bkgql,blkd->bqkgd/dot_general | solution.py:172
  107.3 5.3 all-to-all-start
  116.8 22.2 %all-to-all-done = bf16[8,64,2048]{2,1,0:T(8,128)(2,1)} async-done(((bf16[8,64,2048]{2,1,0:T(8,128)(2,1)}), bf16[8,64,2048]{2,1,0:T(8,128)(2,1)}, u32[]{:S(2)}, u32[]{:S(2)}) %all-to-all-start) | async-done | bytes 2097184 | tf_op jit(solution)/shard_map/all_to_all | solution.py:26
  155.3 21.0 %all-to-all-done.1 = bf16[8,64,2048]{2,1,0:T(8,128)(2,1)} async-done(((bf16[8,64,2048]{2,1,0:T(8,128)(2,1)}), bf16[8,64,2048]{2,1,0:T(8,128)(2,1)}, u32[]{:S(2)}, u32[]{:S(2)}) %all-to-all-start.1) | async-done | bytes 2097184 | tf_op jit(solution)/shard_map/all_to_all | solution.py:32
  202.2 22.2 %all-to-all-done.4 = bf16[8,64,2048]{2,1,0:T(8,128)(2,1)} async-done(((bf16[8,64,2048]{2,1,0:T(8,128)(2,1)}), bf16[8,64,2048]{2,1,0:T(8,128)(2,1)}, u32[]{:S(2)}, u32[]{:S(2)}) %all-to-all-start.4) | async-done | bytes 2097184 | tf_op jit(solution)/shard_map/all_to_all | solution.py:26
  231.9 23.3 %all-to-all-done.2 = bf16[8,64,2048]{2,1,0:T(8,128)(2,1)S(1)} async-done(((bf16[8,64,2048]{2,1,0:T(8,128)(2,1)}), bf16[8,64,2048]{2,1,0:T(8,128)(2,1)S(1)}, u32[]{:S(2)}, u32[]{:S(2)}) %all-to-all-start.2) | async-done | bytes 2097184 | tf_op jit(solution)/shard_map/all_to_all | solution.py:26
  258.0 29.9 %all_to_all.40 = bf16[8,64,2048]{2,1,0:T(8,128)(2,1)S(1)} all-to-all(bf16[8,64,2048]{2,1,0:T(8,128)(2,1)S(1)} %broadcast_in_dim.28), channel_id=1, replica_groups=mesh['seq_0'=4,'seq_1'=4,'grp_0'=4,'grp_1'=2] {'grp_0','grp_1'}, dimensions={0} | all-to-all | bytes 4194304 | tf_op jit(solution)/shard_map/all_to_all | solution.py:32
  290.6 8.8 %fusion.11 = bf16[2,4096,1,128]{3,1,0,2:T(8,128)(2,1)} fusion(f32[2,256,2,128]{1,3,2,0:T(8,128)S(1)} %get-tuple-element.80, f32[2,256,2]{1,2,0:T(2,128)S(1)} %fusion.23, f32[2,4096,256,2]{2,1,3,0:T(8,128)} %copy-done.2, f32[2,2,256]{2,1,0:T(2,128)S(1)} %log_add_fusion, pred[2,256,4096]{1,2,0:T(8,128)(4,1)S(1)} %copy-done.8), kind=kOutput, calls=%fused_computation.18 | convolution fusion | flops 1091829760 | bytes 21504000 | tf_op jit(solution)/shard_map/bkgql,bqkgd->blkd/dot_general | solution.py:245
  299.4 12.2 %fusion = (f32[2,2,256]{2,1,0:T(2,128)S(1)}, f32[2,4096,256,2]{2,1,3,0:T(8,128)}) fusion(f32[2,4096,256,2]{2,1,3,0:T(8,128)} %copy-done.2, f32[2,2,256]{2,1,0:T(2,128)S(1)} %log_add_fusion, pred[2,256,4096]{1,2,0:T(8,128)(4,1)S(1)} %copy-done.8, f32[2,256,2,128]{1,3,2,0:T(8,128)S(1)} %get-tuple-element.80, f32[2,256,2]{1,2,0:T(2,128)S(1)} %fusion.23, ...), kind=kOutput, calls=%fused_computation.3 | convolution fusion | flops 1094974464 | bytes 38285312 | tf_op jit(solution)/shard_map/bqkgd,blkd->bkgql/dot_general | solution.py:232
  311.6 12.2 %fusion.6 = bf16[2,2,256,4096]{2,3,1,0:T(8,128)(2,1)S(1)} fusion(f32[2,4096,256,2]{2,1,3,0:T(8,128)} %get-tuple-element.78, f32[2,4096,256,2]{2,1,3,0:T(8,128)} %copy-done.2, f32[2,2,256]{2,1,0:T(2,128)S(1)} %get-tuple-element.77, f32[2,2,256]{2,1,0:T(2,128)S(1)} %log_add_fusion, pred[2,256,4096]{1,2,0:T(8,128)(4,1)S(1)} %copy-done.8), kind=kLoop, calls=%fused_computation.11 | loop fusion | flops 25165824 | bytes 44048384 | tf_op jit(solution)/shard_map/reshape.48
  334.4 5.3 convolution_convert_fusion.1
  339.7 5.2 convolution_convert_fusion.2
  356.1 49.8 %reduce-scatter.2.cloned.1.call-done = bf16[4,256,1,128]{3,1,0,2:T(8,128)(2,1)} async-done(((bf16[4,4096,1,128]{3,1,0,2:T(8,128)(2,1)}), bf16[4,256,1,128]{3,1,0,2:T(8,128)(2,1)}) %reduce-scatter.2.cloned.1.call-update) | async-done | bytes 262160 | tf_op jit(solution)/shard_map/reduce_scatter | solution.py:57
  417.5 33.3 %all_to_all.41 = bf16[8,64,2048]{2,1,0:T(8,128)(2,1)} all-to-all(bf16[8,64,2048]{2,1,0:T(8,128)(2,1)S(1)} %bitcast.242), channel_id=1, replica_groups=mesh['seq_0'=4,'seq_1'=4,'grp_0'=4,'grp_1'=2] {'grp_0','grp_1'}, dimensions={0} | all-to-all | bytes 4194304 | tf_op jit(solution)/shard_map/all_to_all | solution.py:26
  452.4 5.4 all-to-all-start.3
  462.4 21.8 %all-to-all-done.3 = bf16[8,64,2048]{2,1,0:T(8,128)(2,1)} async-done(((bf16[8,64,2048]{2,1,0:T(8,128)(2,1)}), bf16[8,64,2048]{2,1,0:T(8,128)(2,1)}, u32[]{:S(2)}, u32[]{:S(2)}) %all-to-all-start.3) | async-done | bytes 2097184 | tf_op jit(solution)/shard_map/all_to_all | solution.py:32
  491.4 32.3 %psum.175 = bf16[2048,2]{0,1:T(2,128)(2,1)S(1)} all-reduce(bf16[2048,2]{0,1:T(2,128)(2,1)S(1)} %fusion.12), channel_id=1, replica_groups=mesh['seq_0'=4,'seq_1'=4,'grp_0'=4,'grp_1'=2] {'seq_0','seq_1'}, use_global_device_ids=true, to_apply=%region_26.27 | all-reduce | flops 4096 | bytes 16384 | tf_op jit(solution)/shard_map/psum | solution.py:305
  524.3 11.3 %all-reduce.2 = (f32[2048]{0:T(1024)S(1)}, f32[128]{0:T(128)S(1)}, f32[128]{0:T(128)S(1)}, f32[2048]{0:T(1024)S(1)}) all-reduce(f32[2048]{0:T(1024)S(1)} %get-tuple-element.14, f32[128]{0:T(128)S(1)} %copy-done.61, f32[128]{0:T(128)S(1)} %copy-done.62, ...), channel_id=1, replica_groups=mesh['seq_0'=4,'seq_1'=4,'grp_0'=4,'grp_1'=2] {'seq_0'}, use_global_device_ids=true, to_apply=%region_19.20 | all-reduce | flops 4352 | bytes 34816 | tf_op jit(solution)/shard_map/psum | solution.py:65
  535.7 12.0 %all-reduce.1 = (f32[2048]{0:T(1024)S(1)}, f32[128]{0:T(128)S(1)}, f32[128]{0:T(128)S(1)}, f32[2048]{0:T(1024)S(1)}) all-reduce(f32[2048]{0:T(1024)S(1)} %get-tuple-element.30, f32[128]{0:T(128)S(1)} %get-tuple-element.31, f32[128]{0:T(128)S(1)} %get-tuple-element.32, ...), channel_id=1, replica_groups=mesh['seq_0'=4,'seq_1'=4,'grp_0'=4,'grp_1'=2] {'seq_1'}, use_global_device_ids=true, to_apply=%region_20.21 | all-reduce | flops 4352 | bytes 34816 | tf_op jit(solution)/shard_map/psum | solution.py:65
  547.7 15.1 %all-reduce = (f32[2048]{0:T(1024)S(1)}, f32[128]{0:T(128)S(1)}, f32[128]{0:T(128)S(1)}, f32[2048]{0:T(1024)S(1)}) all-reduce(f32[2048]{0:T(1024)S(1)} %get-tuple-element.26, f32[128]{0:T(128)S(1)} %get-tuple-element.27, f32[128]{0:T(128)S(1)} %get-tuple-element.28, ...), channel_id=1, replica_groups=mesh['seq_0'=4,'seq_1'=4,'grp_0'=4,'grp_1'=2] {'grp_0'}, use_global_device_ids=true, to_apply=%region_21.22 | all-reduce | flops 4352 | bytes 34816 | tf_op jit(solution)/shard_map/psum | solution.py:65
  562.8 19.2 %all-reduce.3 = (f32[2048]{0:T(1024)}, f32[128]{0:T(128)}, f32[128]{0:T(128)}, f32[2048]{0:T(1024)}) all-reduce(f32[2048]{0:T(1024)S(1)} %get-tuple-element.22, f32[128]{0:T(128)S(1)} %get-tuple-element.23, f32[128]{0:T(128)S(1)} %get-tuple-element.24, ...), channel_id=1, replica_groups=mesh['seq_0'=4,'seq_1'=4,'grp_0'=4,'grp_1'=2] {'grp_1'}, use_global_device_ids=true, to_apply=%region_22.23 | all-reduce | flops 4352 | bytes 34816 | tf_op jit(solution)/shard_map/psum | solution.py:65
  581.9 13.3 %all-reduce.7.cloned.1.call-done = (bf16[2048,256]{1,0:T(8,128)(2,1)}, bf16[2048,128]{1,0:T(8,128)(2,1)}, bf16[2048,128]{1,0:T(8,128)(2,1)}, bf16[256,2048]{1,0:...) async-done(((bf16[2048,256]{1,0:T(8,128)(2,1)}, bf16[2048,128]{1,0:T(8,128)(2,1)}, bf16[2048,128]{1,0:T(8,128)(2,1)}, ...) | async-done | bytes 12582928 | tf_op jit(solution)/shard_map/psum | solution.py:302
  595.2 5.2 convert_element_type.256
  (258 shorter events, 174.9 us)
Async XLA Ops:
  7.2 177.2 %copy-start = (bf16[768,2048]{1,0:T(8,128)(2,1)S(1)}, bf16[768,2048]{1,0:T(8,128)(2,1)}, u32[]{:S(2)}) copy-start(bf16[768,2048]{1,0:T(8,128)(2,1)} %param.28) | copy-start | bytes 9437188
  7.2 71.5 %all-gather.2.cloned.1.call-start = ((), (), s32[]{:S(2)}) async-start(), calls=%async_computation.9 | async-start | bytes 4456448 | tf_op jit(solution)/shard_map/all_gather | solution.py:52
  107.3 31.7 %all-to-all-start = ((bf16[8,64,2048]{2,1,0:T(8,128)(2,1)}), bf16[8,64,2048]{2,1,0:T(8,128)(2,1)}, u32[]{:S(2)}, u32[]{:S(2)}) async-start(bf16[8,64,2048]{2,1,0:T(8,128)(2,1)} %bitcast.245), calls=%async_computation | async-start | bytes 4194304 | tf_op jit(solution)/shard_map/all_to_all | solution.py:26
  116.8 26.3 %copy-start.51 = (f32[2048]{0:T(1024)S(1)}, f32[2048]{0:T(1024)}, u32[]{:S(2)}) copy-start(f32[2048]{0:T(1024)} %param.25) | copy-start | bytes 24580
  144.8 31.6 %all-to-all-start.1 = ((bf16[8,64,2048]{2,1,0:T(8,128)(2,1)}), bf16[8,64,2048]{2,1,0:T(8,128)(2,1)}, u32[]{:S(2)}, u32[]{:S(2)}) async-start(bf16[8,64,2048]{2,1,0:T(8,128)(2,1)} %broadcast_in_dim.26), calls=%async_computation.1 | async-start | bytes 4194304 | tf_op jit(solution)/shard_map/all_to_all | solution.py:32
  192.8 31.6 %all-to-all-start.4 = ((bf16[8,64,2048]{2,1,0:T(8,128)(2,1)}), bf16[8,64,2048]{2,1,0:T(8,128)(2,1)}, u32[]{:S(2)}, u32[]{:S(2)}) async-start(bf16[8,64,2048]{2,1,0:T(8,128)(2,1)} %bitcast.256), calls=%async_computation.4 | async-start | bytes 4194304 | tf_op jit(solution)/shard_map/all_to_all | solution.py:26
  224.4 30.9 %all-to-all-start.2 = ((bf16[8,64,2048]{2,1,0:T(8,128)(2,1)}), bf16[8,64,2048]{2,1,0:T(8,128)(2,1)S(1)}, u32[]{:S(2)}, u32[]{:S(2)}) async-start(bf16[8,64,2048]{2,1,0:T(8,128)(2,1)} %bitcast.255), calls=%async_computation.2 | async-start | bytes 4194304 | tf_op jit(solution)/shard_map/all_to_all | solution.py:26
  228.9 177.1 %reduce-scatter.2.cloned.1.call-start = ((), (), s32[]{:S(2)}) async-start(), calls=%async_computation.10 | async-start | bytes 4456448 | tf_op jit(solution)/shard_map/reduce_scatter | solution.py:57
  257.7 31.5 %copy-start.36 = (bf16[256,2048]{1,0:T(8,128)(2,1)S(1)}, bf16[256,2048]{1,0:T(8,128)(2,1)}, u32[]{:S(2)}) copy-start(bf16[256,2048]{1,0:T(8,128)(2,1)} %param.24) | copy-start | bytes 3145732
  257.7 31.5 %copy-start.45 = (f32[2,128,2,256]{3,1,2,0:T(8,128)S(1)}, f32[2,128,2,256]{3,1,2,0:T(8,128)}, u32[]{:S(2)}) copy-start(f32[2,128,2,256]{3,1,2,0:T(8,128)} %get-tuple-element.82) | copy-start | bytes 1572868
  311.6 15.5 %copy-start.48 = (bf16[2,256,2,64]{1,3,2,0:T(8,128)(2,1)S(1)}, bf16[2,256,2,64]{1,3,2,0:T(8,128)(2,1)}, u32[]{:S(2)}) copy-start(bf16[2,256,2,64]{1,3,2,0:T(8,128)(2,1)} %get-tuple-element.56) | copy-start | bytes 393220
  311.6 15.5 %copy-start.49 = (bf16[2,256,2,64]{1,3,2,0:T(8,128)(2,1)S(1)}, bf16[2,256,2,64]{1,3,2,0:T(8,128)(2,1)}, u32[]{:S(2)}) copy-start(bf16[2,256,2,64]{1,3,2,0:T(8,128)(2,1)} %get-tuple-element.57) | copy-start | bytes 393220
  332.0 263.2 %all-reduce.7.cloned.1.call-start = ((), (), s32[]{:S(2)}) async-start(), calls=%async_computation.11 | async-start | bytes 25165824 | tf_op jit(solution)/shard_map/psum | solution.py:302
  334.4 14.0 %slice-start = ((s8[8388608]{0:T(1024)(128)(4,1)}), s8[4194304]{0:T(1024)(128)(4,1)S(1)}, s32[]{:S(2)}) async-start(s8[8388608]{0:T(1024)(128)(4,1)} %bitcast.240), calls=%async_computation.12 | async-start | bytes 8388608
  354.4 52.7 %copy-start.31 = (f32[256,64]{1,0:T(8,128)S(1)}, f32[256,64]{1,0:T(8,128)}, u32[]{:S(2)}) copy-start(f32[256,64]{1,0:T(8,128)} %copy-done.30) | copy-start | bytes 196612
  354.4 52.7 %copy-start.44 = (f32[256,64]{1,0:T(8,128)S(1)}, f32[256,64]{1,0:T(8,128)}, u32[]{:S(2)}) copy-start(f32[256,64]{1,0:T(8,128)} %copy.59) | copy-start | bytes 196612
  354.4 52.9 %copy-start.56 = (f32[512]{0:T(512)S(1)}, f32[512]{0:T(512)}, u32[]{:S(2)}) copy-start(f32[512]{0:T(512)} %copy-done.55) | copy-start | bytes 6148
  417.5 33.3 %copy-start.35 = (bf16[64,2048]{1,0:T(8,128)(2,1)S(1)}, bf16[64,2048]{1,0:T(8,128)(2,1)}, u32[]{:S(2)}) copy-start(bf16[64,2048]{1,0:T(8,128)(2,1)} %get-tuple-element.60) | copy-start | bytes 786436
  452.4 8.8 %copy-start.26 = (f32[64,2048]{1,0:T(8,128)S(1)}, f32[64,2048]{1,0:T(8,128)}, u32[]{:S(2)}) copy-start(f32[64,2048]{1,0:T(8,128)} %get-tuple-element.46) | copy-start | bytes 1572868
  452.4 31.9 %all-to-all-start.3 = ((bf16[8,64,2048]{2,1,0:T(8,128)(2,1)}), bf16[8,64,2048]{2,1,0:T(8,128)(2,1)}, u32[]{:S(2)}, u32[]{:S(2)}) async-start(bf16[8,64,2048]{2,1,0:T(8,128)(2,1)} %broadcast_in_dim.27), calls=%async_computation.3 | async-start | bytes 4194304 | tf_op jit(solution)/shard_map/all_to_all | solution.py:32
  485.8 38.5 %copy-start.54 = (f32[2048]{0:T(1024)S(1)}, f32[2048]{0:T(1024)}, u32[]{:S(2)}) copy-start(f32[2048]{0:T(1024)} %get-tuple-element.18) | copy-start | bytes 24580
  485.8 38.5 %copy-start.61 = (f32[128]{0:T(128)S(1)}, f32[128]{0:T(128)}, u32[]{:S(2)}) copy-start(f32[128]{0:T(128)} %get-tuple-element.16) | copy-start | bytes 1540
  485.8 38.5 %copy-start.62 = (f32[128]{0:T(128)S(1)}, f32[128]{0:T(128)}, u32[]{:S(2)}) copy-start(f32[128]{0:T(128)} %get-tuple-element.20) | copy-start | bytes 1540
  485.8 96.1 %all-to-all-start.7 = ((bf16[8,64,2048]{2,1,0:T(8,128)(2,1)}), bf16[8,64,2048]{2,1,0:T(8,128)(2,1)}, u32[]{:S(2)}, u32[]{:S(2)}) async-start(bf16[8,64,2048]{2,1,0:T(8,128)(2,1)} %broadcast_in_dim.29), calls=%async_computation.8 | async-start | bytes 4194304 | tf_op jit(solution)/shard_map/all_to_all | solution.py:32
  (59 other events, 204.6 us)
Sparse Core Ops, SparseCore 0:
  24.1 54.5 all-gather.1
  332.1 73.8 reduce-scatter.1
  413.0 182.1 all-reduce.6
where the time goes:
time: 630 us; the launch traced here: 626 us
  waiting for transfers between devices  211 us (33%)
  blocking collectives  153 us (24%)
  matrix products  96.7 us (15%)
  other arithmetic  81.9 us (13%)
  local copies, waits for them, and re-layouts  36 us (6%)
  starting transfers between devices  31.4 us (5%)
  between operations  15.4 us (2%)
    all_to_all x3, waiting for transfers between devices, sent_and_summed(): lax.all_to_all(in_blocks(value, dim, count), axis, 0, 0, tiled=True)  67.8 us
    psum x4, blocking collectives, by_axis(): return functools.reduce(lax.psum, axes, value)  57.6 us
    reduce_scatter x1, waiting for transfers between devices, sent_together_2(): lax.psum_scatter(both, axis, scatter_dimension=dim, tiled=True)  49.8 us
    all_to_all x3, waiting for transfers between devices, sent_to_all(): return lax.all_to_all(copies, axis, split_axis=0, concat_axis=0, tiled=True)  42.8 us
    all_gather x1, waiting for transfers between devices, sent_together(): lax.all_gather(both, axis, axis=dim, tiled=True)  37.5 us
    all_to_all x1, blocking collectives, sent_and_summed(): lax.all_to_all(in_blocks(value, dim, count), axis, 0, 0, tiled=True)  33.3 us
    psum x1, blocking collectives, local(): lax.psum(grad_w_gate.astype(jnp.bfloat16), SEQ).astype(jnp.float32)  32.3 us
    all_to_all x1, blocking collectives, sent_to_all(): return lax.all_to_all(copies, axis, split_axis=0, concat_axis=0, tiled=True)  29.9 us
  transfers between devices with their start and end apart: 9, of which 8 were waited for; matrix products, arithmetic and copies ran while one was open for 11% of the time, Pallas kernels for 0%

commit v1 on v0

v1 whole, which is shorter than its diff:
```python
import functools

import jax
import jax.numpy as jnp
import numpy as np
from jax import lax
from jax.experimental import pallas as pl
from jax.experimental.pallas import tpu as pltpu
from jax.sharding import Mesh
from jax.sharding import PartitionSpec as P

GRP = ("grp_0", "grp_1")
SEQ = ("seq_0", "seq_1")
SEQ_GRP = ("seq_0", "seq_1", "grp_0", "grp_1")
MESH = pl.DeviceIdType.MESH
VMEM_LIMIT = 56 * 2**20

f32 = jnp.float32
bf16 = jnp.bfloat16


epsilon = 1e-06
rope_base = 1000000.0


def unit_scale(values):
    inverse = lax.rsqrt(jnp.mean(values * values, axis=-1, keepdims=True) + epsilon)
    return (values * inverse, inverse)


def norm_back(grad_unit, unit, inverse):
    return inverse * (grad_unit - unit * jnp.mean(grad_unit * unit, axis=-1, keepdims=True))


ROW_CONTRACT = (((1,), (1,)), ((), ()))
COL_CONTRACT = (((0,), (0,)), ((), ()))


def send(source, target, sems, slot, to):
    copy = pltpu.make_async_remote_copy(
        src_ref=source,
        dst_ref=target,
        send_sem=sems.at[0, slot],
        recv_sem=sems.at[1, slot],
        device_id=to,
        device_id_type=MESH,
    )
    copy.start()
    return copy


def group_places():
    z = lax.axis_index("grp_0")
    core = lax.axis_index("grp_1")
    ring = lax.axis_size("grp_0")
    above = {"grp_0": lax.rem(z + 1, ring)}
    below = {"grp_0": lax.rem(z + ring - 1, ring)}
    twin = {"grp_1": 1 - core}
    return z, core, above, below, twin


def greet(places):
    barrier = pltpu.get_barrier_semaphore()
    for place in places:
        pl.semaphore_signal(barrier, inc=1, device_id=place, device_id_type=MESH)
    return lambda: pl.semaphore_wait(barrier, len(places))


def group_rows(z, core, far, share):
    return pl.multiple_of((lax.rem(z + far, 4) * 2 + core) * share, share)


FAR = (2, 1, 3, 0)


def sum_rows(product, share, ready, scratch):
    mine, twin_out, twin_in, low, ring, twin_sems, ring_sems = scratch
    z, core, above, below, twin = group_places()
    half = share // 2
    top, bottom = pl.ds(0, half), pl.ds(half, half)

    def put_twin(cols, block):
        twin_out[:, :, cols] = block.astype(bf16)

    def put_mine(cols, block):
        mine[:, :, cols] = block

    product(1 - core, put_twin)
    ready()
    pairs = [send(twin_out.at[k], twin_in.at[k], twin_sems, k, twin) for k in range(4)]
    product(core, put_mine)

    def joined(k, rows):
        return mine[k, rows, :] + twin_in[k, rows, :].astype(f32)

    pairs[0].wait_recv()
    low[0] = joined(0, pl.ds(0, share)).astype(bf16)
    steps = [
        send(low.at[0, top], ring.at[0], ring_sems, 0, above),
        send(low.at[0, bottom], ring.at[1], ring_sems, 1, below),
    ]
    pairs[1].wait_recv()
    low[1, bottom, :] = joined(1, bottom).astype(bf16)
    steps.append(send(low.at[1, bottom], ring.at[2], ring_sems, 2, above))
    pairs[2].wait_recv()
    low[2, top, :] = joined(2, top).astype(bf16)
    steps.append(send(low.at[2, top], ring.at[3], ring_sems, 3, below))
    steps[0].wait_recv()
    low[1, top, :] = (joined(1, top) + ring[0].astype(f32)).astype(bf16)
    steps.append(send(low.at[1, top], ring.at[4], ring_sems, 4, above))
    steps[1].wait_recv()
    low[2, bottom, :] = (joined(2, bottom) + ring[1].astype(f32)).astype(bf16)
    steps.append(send(low.at[2, bottom], ring.at[5], ring_sems, 5, below))
    pairs[3].wait_recv()
    for step in steps[2:]:
        step.wait_recv()
    total = jnp.concatenate(
        [
            joined(3, top) + ring[3].astype(f32) + ring[4].astype(f32),
            joined(3, bottom) + ring[2].astype(f32) + ring[5].astype(f32),
        ],
        axis=0,
    )
    return total, pairs + steps


def join_rows(whole, share, twin_sems, ring_sems):
    z, core, above, below, twin = group_places()
    half = share // 2

    def part(far, side):
        start = group_rows(z, core, far, share)
        return whole.at[pl.ds(pl.multiple_of(start + side * half, half), half), :]

    def hand(far, side, sems, slot, to):
        block = part(far, side)
        return send(block, block, sems, slot, to)

    own = whole.at[pl.ds(group_rows(z, core, 0, share), share), :]
    up = [hand(0, 0, ring_sems, 0, above), hand(0, 1, ring_sems, 1, above)]
    down = [hand(0, 1, ring_sems, 2, below), hand(0, 0, ring_sems, 3, below)]
    across = [send(own, own, twin_sems, 0, twin)]
    up[0].wait_recv()
    up.append(hand(3, 0, ring_sems, 4, above))
    across.append(hand(3, 0, twin_sems, 1, twin))
    down[0].wait_recv()
    down.append(hand(1, 1, ring_sems, 5, below))
    across.append(hand(1, 1, twin_sems, 2, twin))
    up[1].wait_recv()
    across.append(hand(3, 1, twin_sems, 3, twin))
    down[1].wait_recv()
    across.append(hand(1, 0, twin_sems, 4, twin))
    up[2].wait_recv()
    across.append(hand(2, 0, twin_sems, 5, twin))
    down[2].wait_recv()
    across.append(hand(2, 1, twin_sems, 6, twin))
    for copy in across:
        copy.wait_recv()
    for copy in up + down + across:
        copy.wait_send()


def row_scratch(rows, share, width):
    return [
        pltpu.VMEM((4, share, width), f32),
        pltpu.VMEM((4, share, width), bf16),
        pltpu.VMEM((4, share, width), bf16),
        pltpu.VMEM((3, share, width), bf16),
        pltpu.VMEM((6, share // 2, width), bf16),
        pltpu.SemaphoreType.DMA((2, 4)),
        pltpu.SemaphoreType.DMA((2, 6)),
        pltpu.VMEM((rows, width), bf16),
        pltpu.SemaphoreType.DMA((2, 7)),
        pltpu.SemaphoreType.DMA((2, 6)),
        pltpu.SemaphoreType.DMA((1,)),
    ]


def group_product(lefts, rights, across, share, width):
    z = lax.axis_index("grp_0")
    step = 512

    def product(core, put):
        picked = []
        for left in lefts:
            blocks = [left[pl.ds(group_rows(z, core, far, share), share), :] for far in FAR]
            picked.append(jnp.concatenate(blocks, axis=0))
        for at in range(0, width, step):
            cols = pl.ds(at, step)
            total = None
            for left, right in zip(picked, rights):
                if across:
                    term = lax.dot_general(
                        left, right[cols, :], ROW_CONTRACT, preferred_element_type=f32
                    )
                else:
                    term = jnp.dot(left, right[:, cols], preferred_element_type=f32)
                total = term if total is None else total + term
            put(cols, total.reshape(4, share, step))

    return product


def row_kernel(n_pairs, across, finish, n_extra, n_out, share, width, *refs):
    lefts = refs[:n_pairs]
    rights = refs[n_pairs : 2 * n_pairs]
    extra = refs[2 * n_pairs : 2 * n_pairs + n_extra]
    at = 2 * n_pairs + n_extra
    outs = refs[at : at + n_out]
    whole_out = refs[at + n_out]
    scratch = refs[at + n_out + 1 :]
    z, core, above, below, twin = group_places()
    ready = greet((above, below, twin))
    product = group_product(lefts, rights, across, share, width)
    total, copies = sum_rows(product, share, ready, scratch[:7])
    whole, twin_sems, ring_sems, out_sem = scratch[7:]
    whole[pl.ds(group_rows(z, core, 0, share), share), :] = finish(total, extra, outs)
    for copy in copies:
        copy.wait_send()
    join_rows(whole, share, twin_sems, ring_sems)
    done = pltpu.make_async_copy(whole, whole_out, out_sem.at[0])
    done.start()
    done.wait()


def exchange_rows(name, call_id, lefts, rights, across, finish, extra, out_shapes):
    rows = lefts[0].shape[0]
    share = rows // 8
    width = rights[0].shape[0 if across else 1]
    vmem = pl.BlockSpec(memory_space=pltpu.VMEM)
    body = functools.partial(
        row_kernel, len(lefts), across, finish, len(extra), len(out_shapes), share, width
    )
    flops = 2 * rows * width * sum(left.shape[1] for left in lefts)
    return pl.pallas_call(
        body,
        name=name,
        out_shape=tuple(out_shapes) + (jax.ShapeDtypeStruct((rows, width), bf16),),
        in_specs=[vmem] * (2 * len(lefts) + len(extra)),
        out_specs=(vmem,) * len(out_shapes) + (pl.BlockSpec(memory_space=pl.ANY),),
        scratch_shapes=row_scratch(rows, share, width),
        compiler_params=pltpu.CompilerParams(
            collective_id=call_id, has_side_effects=True, vmem_limit_bytes=VMEM_LIMIT
        ),
        cost_estimate=pl.CostEstimate(
            flops=flops, bytes_accessed=16 * 2**20, transcendentals=0
        ),
    )(*lefts, *rights, *extra)


def finish_middle(total, extra, outs):
    base, gain = extra
    middle_out, scale_out = outs
    middle = base[...].astype(f32) + total
    unit, inverse = unit_scale(middle)
    middle_out[...] = middle
    scale_out[...] = inverse
    return (unit * gain[...]).astype(bf16)


def finish_plain(total, extra, outs):
    return (extra[0][...] + total).astype(bf16)


def finish_grad_middle(total, extra, outs):
    middle, inverse, gain, seed = extra
    grad_out, gain_out = outs
    unit = middle[...] * inverse[...]
    gain_out[...] = jnp.sum(total * unit, axis=0, keepdims=True)
    grad = seed[...] + norm_back(total * gain[...], unit, inverse[...])
    grad_out[...] = grad
    return grad.astype(bf16)


def finish_grad_tokens(total, extra, outs):
    base, gain, grad_middle = extra
    (gain_out,) = outs
    unit, inverse = unit_scale(base[...].astype(f32))
    gain_out[...] = jnp.sum(total * unit, axis=0, keepdims=True)
    return (grad_middle[...] + norm_back(total * gain[...], unit, inverse)).astype(bf16)


def feed_kernel(
    rows_ref,
    seed_ref,
    gate_ref,
    up_ref,
    down_ref,
    hidden_out,
    grad_gate_out,
    grad_up_out,
    w_down_out,
    w_gate_out,
    w_up_out,
    rows_across,
):
    @pl.when(pl.program_id(0) == 0)
    def _():
        rows_across[...] = rows_ref[...].T

    rows = rows_ref[...]
    seed = seed_ref[...]
    gate_pre = jnp.dot(rows, gate_ref[...], preferred_element_type=f32)
    up_proj = jnp.dot(rows, up_ref[...], preferred_element_type=f32)
    grad_hidden = lax.dot_general(seed, down_ref[...], ROW_CONTRACT, preferred_element_type=f32)
    gate_sig = jax.nn.sigmoid(gate_pre)
    silu = gate_pre * gate_sig
    hidden = (silu * up_proj).astype(bf16)
    grad_gate = (grad_hidden * up_proj * gate_sig * (1.0 + gate_pre * (1.0 - gate_sig))).astype(
        bf16
    )
    grad_up = (grad_hidden * silu).astype(bf16)
    hidden_out[...] = hidden
    grad_gate_out[...] = grad_gate
    grad_up_out[...] = grad_up
    w_down_out[...] = lax.dot_general(
        hidden, seed, COL_CONTRACT, preferred_element_type=f32
    ).astype(bf16)
    w_gate_out[...] = jnp.dot(rows_across[...], grad_gate, preferred_element_type=f32).astype(bf16)
    w_up_out[...] = jnp.dot(rows_across[...], grad_up, preferred_element_type=f32).astype(bf16)


def feed_forward(rows, seed, w_gate, w_up, w_down):
    count, width = rows.shape
    units = w_gate.shape[1]
    step = 256
    whole = pl.BlockSpec((count, width), lambda j: (0, 0))
    cols = pl.BlockSpec((width, step), lambda j: (0, j))
    strip = pl.BlockSpec((step, width), lambda j: (j, 0))
    narrow = pl.BlockSpec((count, step), lambda j: (0, j))
    thin = jax.ShapeDtypeStruct((count, units), bf16)
    return pl.pallas_call(
        feed_kernel,
        name="feed_forward",
        grid=(units // step,),
        in_specs=[whole, whole, cols, cols, strip],
        out_specs=(narrow, narrow, narrow, strip, cols, cols),
        out_shape=(
            thin,
            thin,
            thin,
            jax.ShapeDtypeStruct((units, width), bf16),
            jax.ShapeDtypeStruct((width, units), bf16),
            jax.ShapeDtypeStruct((width, units), bf16),
        ),
        scratch_shapes=[pltpu.VMEM((width, count), bf16)],
        compiler_params=pltpu.CompilerParams(vmem_limit_bytes=VMEM_LIMIT),
        cost_estimate=pl.CostEstimate(
            flops=12 * count * width * units, bytes_accessed=24 * 2**20, transcendentals=0
        ),
    )(rows, seed, w_gate, w_up, w_down)


LOG2_E = 1.4426950408889634
STAGES = (
    ((1, 0), (3, 0), (0, 1), (0, 3)),
    ((2, 0), (0, 2)),
    ((1, 1), (1, 3), (3, 1), (3, 3)),
    ((1, 2), (3, 2), (2, 1), (2, 3)),
    ((2, 2),),
)


def angle_tables(block, size, count):
    half = size // 2
    freq = rope_base ** (-np.arange(half, dtype=np.float64) * (2.0 / size))
    inner = np.arange(block)[:, None] * freq[None, :]
    outer = (np.arange(count) * block)[:, None] * freq[None, :]

    def table(angle):
        sine = np.sin(angle)
        cosine = np.cos(angle)
        both = np.stack(
            [
                np.concatenate([cosine, cosine], axis=1),
                np.concatenate([-sine, sine], axis=1),
            ]
        )
        return both.astype(np.float32)

    return table(inner), table(outer)


def local_angles(inner, outer, place):
    cos_in, sin_in = inner[0], inner[1]
    cos_out = outer[0, pl.ds(place, 1), :]
    sin_out = outer[1, pl.ds(place, 1), :]
    return cos_in * cos_out - sin_in * sin_out, sin_in * cos_out + cos_in * sin_out


def turned(values):
    return pltpu.roll(values, values.shape[-1] // 2, axis=values.ndim - 1)


def plane_place():
    return lax.axis_index("seq_0"), lax.axis_index("seq_1")


def plane_sides(axis):
    at = lax.axis_index(axis)
    size = lax.axis_size(axis)
    return {axis: lax.rem(at + 1, size)}, {axis: lax.rem(at + size - 1, size)}


AXES = (("seq_1", "seq_0"), ("seq_0", "seq_1"))


def place_at(path, first, second):
    y, x = plane_place()
    dx, dy = (first, second) if path == 0 else (second, first)
    return lax.rem(y + dy, 4) * 4 + lax.rem(x + dx, 4)


def pass_start(block, axis, sems, slot):
    up, down = plane_sides(axis)
    return [send(block, block, sems, slot, up), send(block, block, sems, slot + 1, down)]


def pass_on(copies, before, after, axis, sems, slot):
    up, down = plane_sides(axis)
    copies[0].wait_recv()
    copies.append(send(before.at[0], before.at[0], sems, slot + 2, up))
    copies[1].wait_recv()
    copies.append(send(after.at[1], after.at[1], sems, slot + 3, down))


def pass_end(copies):
    copies[2].wait_recv()
    copies[3].wait_recv()


class Gather:
    def __init__(self, buffer, sems):
        self.buffer, self.sems = buffer, sems
        self.rings = [{}, {}]

    def block(self, path, first, second):
        return self.buffer.at[place_at(path, first, second), path]

    def slot(self, path, ring):
        return path * 20 + (4 if ring == "first" else ring) * 4

    def begin(self, path, ring):
        axis = AXES[path][0] if ring == "first" else AXES[path][1]
        block = self.block(path, 0 if ring == "first" else ring, 0)
        self.rings[path][ring] = pass_start(block, axis, self.sems, self.slot(path, ring))

    def forward(self, path, ring):
        if ring == "first":
            axis, before, after = AXES[path][0], self.block(path, 3, 0), self.block(path, 1, 0)
        else:
            axis = AXES[path][1]
            before, after = self.block(path, ring, 3), self.block(path, ring, 1)
        pass_on(self.rings[path][ring], before, after, axis, self.sems, self.slot(path, ring))

    def end(self, path, ring):
        pass_end(self.rings[path][ring])

    def start(self):
        for path in (0, 1):
            self.begin(path, "first")
        for path in (0, 1):
            self.begin(path, 0)

    def stage(self, number):
        for path in (0, 1):
            if number == 0:
                self.forward(path, "first")
                self.begin(path, 1)
                self.begin(path, 3)
                self.forward(path, 0)
            elif number == 1:
                self.end(path, "first")
                self.begin(path, 2)
                self.end(path, 0)
            elif number == 2:
                self.forward(path, 1)
                self.forward(path, 3)
            elif number == 3:
                self.end(path, 1)
                self.end(path, 3)
                self.forward(path, 2)
            else:
                self.end(path, 2)

    def finish(self):
        for rings in self.rings:
            for copies in rings.values():
                for copy in copies:
                    copy.wait_send()


class Scatter:
    def __init__(self, buffer, recv, sems):
        self.buffer, self.recv, self.sems = buffer, recv, sems
        self.copies = {}

    def block(self, path, ring, step):
        if ring == 4:
            return self.buffer.at[place_at(path, step, 0), path]
        return self.buffer.at[place_at(path, ring, step), path]

    def sides(self, path, ring):
        return plane_sides(AXES[path][0] if ring == 4 else AXES[path][1])

    def push(self, path, ring, half_ref, slot, to):
        at = (path * 5 + ring) * 6 + slot
        copy = send(half_ref, self.recv.at[path, ring, slot], self.sems, at, to)
        self.copies.setdefault((path, ring), []).append(copy)

    def start(self, path, ring):
        up, down = self.sides(path, ring)
        far = self.block(path, ring, 2)
        self.push(path, ring, far.at[0], 0, up)
        self.push(path, ring, far.at[1], 1, down)
        self.push(path, ring, self.block(path, ring, 1).at[1], 2, up)
        self.push(path, ring, self.block(path, ring, 3).at[0], 3, down)

    def forward(self, path, ring):
        up, down = self.sides(path, ring)
        for slot, step, half, to in ((0, 1, 0, up), (1, 3, 1, down)):
            self.copies[path, ring][slot].wait_recv()
            part = self.block(path, ring, step).at[half]
            came = self.recv[path, ring, slot]
            part[...] = (part[...].astype(f32) + came.astype(f32)).astype(bf16)
            self.push(path, ring, part, slot + 4, to)

    def total(self, path, ring):
        for copy in self.copies[path, ring][2:]:
            copy.wait_recv()
        own = self.block(path, ring, 0)
        out = []
        for half, slots in ((0, (3, 4)), (1, (2, 5))):
            value = own[half].astype(f32)
            for slot in slots:
                value = value + self.recv[path, ring, slot].astype(f32)
            out.append(value)
        return out

    def settle(self, path, ring):
        own = self.block(path, ring, 0)
        for half, value in enumerate(self.total(path, ring)):
            own[half] = value.astype(bf16)

    def finish(self):
        for copies in self.copies.values():
            for copy in copies:
                copy.wait_send()


def greet_plane():
    places = [*plane_sides("seq_0"), *plane_sides("seq_1")]
    return greet(places)


def choose(index, options):
    value = options[-1]
    for n in range(len(options) - 2, -1, -1):
        value = jnp.where(index == n, options[n], value)
    return value


def attend_kernel(
    lengths_ref,
    tokens_ref,
    gain_ref,
    w_query_ref,
    w_key_ref,
    w_value_ref,
    w_gate_ref,
    gain_query_ref,
    gain_key_ref,
    inner_ref,
    outer_ref,
    normed_out,
    query_raw_out,
    key_raw_out,
    logits_out,
    query_out,
    keys_out,
    attended_out,
    lse_out,
    gated_out,
    normed,
    kv,
    sums,
    sems,
    out_sems,
):
    ready = greet_plane()
    y, x = plane_place()
    place = y * 4 + x
    rows, width = tokens_ref.shape
    buckets = kv.shape[1]
    block, size = kv.shape[3], kv.shape[4]
    heads = w_query_ref.shape[1] // size
    step = 64

    def norm_rows(n, carry):
        at = pl.ds(pl.multiple_of(n * step, step), step)
        unit, _ = unit_scale(tokens_ref[at, :].astype(f32))
        normed[at, :] = (unit * gain_ref[...]).astype(bf16)
        return carry

    lax.fori_loop(0, rows // step, norm_rows, 0)
    save_normed = pltpu.make_async_copy(normed, normed_out, out_sems.at[0])
    save_normed.start()
    cosine, sine = local_angles(inner_ref, outer_ref, place)

    def turn(values):
        return values * cosine + turned(values) * sine

    key_raw = jnp.dot(normed[...], w_key_ref[...], preferred_element_type=f32)
    value = jnp.dot(normed[...], w_value_ref[...], preferred_element_type=f32)
    key_raw_out[...] = key_raw
    spots = place * block + lax.broadcasted_iota(jnp.int32, (block, size), 0)
    for b in range(buckets):
        live = spots < lengths_ref[b]
        part = slice(b * block, (b + 1) * block)
        unit, _ = unit_scale(key_raw[part])
        kv[place, b, 0] = jnp.where(live, turn(unit * gain_key_ref[...]), 0.0).astype(bf16)
        kv[place, b, 1] = jnp.where(live, value[part], 0.0).astype(bf16)
    gather = Gather(kv, sems)
    ready()
    gather.start()
    query_raw = jnp.dot(normed[...], w_query_ref[...], preferred_element_type=f32)
    query_raw_out[...] = query_raw
    logits_out[...] = jnp.dot(normed[...], w_gate_ref[...], preferred_element_type=f32)
    for b in range(buckets):
        for h in range(heads):
            part = query_raw[b * block : (b + 1) * block, h * size : (h + 1) * size]
            unit, _ = unit_scale(part)
            query_out[b, h * block : (h + 1) * block, :] = turn(
                unit * gain_query_ref[...]
            ).astype(bf16)
    scale = size**-0.5 * LOG2_E

    def weigh(source, b, causal):
        keys, vals = kv[source, b, 0], kv[source, b, 1]
        scores = lax.dot_general(query_out[b], keys, ROW_CONTRACT, preferred_element_type=f32)
        weights = jnp.exp2(scores * scale)
        if causal:
            spot = lax.broadcasted_iota(jnp.int32, (heads * block, block), 0) % block
            column = lax.broadcasted_iota(jnp.int32, (heads * block, block), 1)
            weights = jnp.where(column <= spot, weights, 0.0)
        there = source * block + lax.broadcasted_iota(jnp.int32, (block, size), 0)
        ones = jnp.where(there < lengths_ref[b], 1.0, 0.0).astype(bf16)
        both = jnp.concatenate([vals, ones], axis=1)
        return jnp.dot(weights.astype(bf16), both, preferred_element_type=f32)

    for b in range(buckets):
        sums[b] = weigh(place, b, True)
    for number, offsets in enumerate(STAGES):
        gather.stage(number)

        def one(n, carry):
            which, b = n // buckets, n % buckets
            dx = choose(which, [o[0] for o in offsets])
            dy = choose(which, [o[1] for o in offsets])
            source = lax.rem(y + dy, 4) * 4 + lax.rem(x + dx, 4)

            @pl.when(source < place)
            def _():
                sums[b] = sums[b] + weigh(source, b, False)

            return carry

        lax.fori_loop(0, len(offsets) * buckets, one, 0)
    save_keys = pltpu.make_async_copy(kv, keys_out, out_sems.at[1])
    save_keys.start()
    gates = jax.nn.sigmoid(logits_out[...])
    for b in range(buckets):
        for h in range(heads):
            at = slice(h * block, (h + 1) * block)
            total = sums[b, at, size:]
            attended = sums[b, at, :size] / total
            here = (slice(b * block, (b + 1) * block), slice(h * size, (h + 1) * size))
            attended_out[here] = attended
            lse_out[b, at, :] = jnp.log2(total)
            gated_out[here] = (attended * gates[here[0], h : h + 1]).astype(bf16)
    gather.finish()
    save_normed.wait()
    save_keys.wait()


def attend(call_id, lengths, tokens, gain, w_query, w_key, w_value, w_gate, gain_q, gain_k, tables):
    rows, width = tokens.shape
    size = gain_q.shape[1]
    buckets = lengths.shape[0]
    block = rows // buckets
    heads = w_query.shape[1] // size
    places = lax.axis_size(SEQ)
    vmem = pl.BlockSpec(memory_space=pltpu.VMEM)
    hbm = pl.BlockSpec(memory_space=pl.ANY)
    shape = jax.ShapeDtypeStruct
    pairs = (places, buckets, 2, block, size)
    return pl.pallas_call(
        attend_kernel,
        name="attend",
        out_shape=(
            shape((rows, width), bf16),
            shape((rows, heads * size), f32),
            shape((rows, size), f32),
            shape((rows, heads), f32),
            shape((buckets, heads * block, size), bf16),
            shape(pairs, bf16),
            shape((rows, heads * size), f32),
            shape((buckets, heads * block, size), f32),
            shape((rows, heads * size), bf16),
        ),
        in_specs=[pl.BlockSpec(memory_space=pltpu.SMEM)] + [vmem] * 10,
        out_specs=(hbm, vmem, vmem, vmem, vmem, hbm, vmem, vmem, vmem),
        scratch_shapes=[
            pltpu.VMEM((rows, width), bf16),
            pltpu.VMEM(pairs, bf16),
            pltpu.VMEM((buckets, heads * block, 2 * size), f32),
            pltpu.SemaphoreType.DMA((2, 40)),
            pltpu.SemaphoreType.DMA((2,)),
        ],
        compiler_params=pltpu.CompilerParams(
            collective_id=call_id, has_side_effects=True, vmem_limit_bytes=VMEM_LIMIT
        ),
        cost_estimate=pl.CostEstimate(
            flops=4 * 2**30, bytes_accessed=16 * 2**20, transcendentals=2**22
        ),
    )(lengths, tokens, gain, w_query, w_key, w_value, w_gate, gain_q, gain_k, *tables)


def back_kernel(
    lengths_ref,
    grad_ref,
    w_out_ref,
    attended_ref,
    logits_ref,
    query_ref,
    lse_ref,
    query_raw_ref,
    key_raw_ref,
    gain_query_ref,
    gain_key_ref,
    inner_ref,
    outer_ref,
    kv_hbm,
    grad_query_out,
    grad_key_out,
    grad_value_out,
    grad_logits_out,
    gain_query_out,
    gain_key_out,
    kv,
    grads,
    recv,
    grad_attended,
    shift,
    delta,
    grad_turned,
    sems,
    in_sems,
):
    ready = greet_plane()
    load = pltpu.make_async_copy(kv_hbm, kv, in_sems.at[0])
    load.start()
    y, x = plane_place()
    place = y * 4 + x
    buckets = kv.shape[1]
    block, size = kv.shape[3], kv.shape[4]
    heads = w_out_ref.shape[0] // size
    grad_gated = lax.dot_general(
        grad_ref[...], w_out_ref[...], ROW_CONTRACT, preferred_element_type=f32
    )
    gates = jax.nn.sigmoid(logits_ref[...])
    for h in range(heads):
        cols = slice(h * size, (h + 1) * size)
        gate = gates[:, h : h + 1]
        part, attended = grad_gated[:, cols], attended_ref[:, cols]
        along = jnp.sum(part * attended, axis=1, keepdims=True)
        grad_logits_out[:, h : h + 1] = (along * gate * (1.0 - gate)).astype(bf16)
        low = (part * gate).astype(bf16)
        inner = jnp.sum(low.astype(f32) * attended, axis=1, keepdims=True)
        wide = jnp.broadcast_to(inner, (inner.shape[0], size))
        for b in range(buckets):
            rows = slice(b * block, (b + 1) * block)
            at = slice(h * block, (h + 1) * block)
            grad_attended[b, at, :] = low[rows]
            delta[b, :, at] = wide[rows].T[:8]
    for b in range(buckets):
        shift[b] = lse_ref[b].T[:8]
    grad_turned[...] = jnp.zeros_like(grad_turned)
    load.wait()
    ready()
    scale = size**-0.5

    def back(source, b, causal):
        keys, vals = kv[source, b, 0], kv[source, b, 1]
        query = query_ref[b]
        given = grad_attended[b]
        scores = lax.dot_general(keys, query, ROW_CONTRACT, preferred_element_type=f32)
        weights = jnp.exp2(scores * (scale * LOG2_E) - shift[b, 0:1, :])
        if causal:
            spot = lax.broadcasted_iota(jnp.int32, (block, heads * block), 1) % block
            key_spot = lax.broadcasted_iota(jnp.int32, (block, heads * block), 0)
            weights = jnp.where(key_spot <= spot, weights, 0.0)
        grad_weights = lax.dot_general(vals, given, ROW_CONTRACT, preferred_element_type=f32)
        grad_scores = (weights * (grad_weights - delta[b, 0:1, :])).astype(bf16)
        grad_keys = jnp.dot(grad_scores, query, preferred_element_type=f32) * scale
        grad_vals = jnp.dot(weights.astype(bf16), given, preferred_element_type=f32)
        grads[source, b, 0] = grad_keys.astype(bf16)
        grads[source, b, 1] = grad_vals.astype(bf16)
        grad_turned[b] += lax.dot_general(
            keys, grad_scores, COL_CONTRACT, preferred_element_type=f32
        )

    def visit(source, b):
        @pl.when(source < place)
        def _():
            back(source, b, False)

        @pl.when(source > place)
        def _():
            grads[source, b] = jnp.zeros_like(grads[source, b])

    scatter = Scatter(grads, recv, sems)
    order = (2, 1, 3, 0)
    for ring in order:
        for path in (0, 1):

            def one(n, carry):
                visit(place_at(path, ring, choose(n, [2, 1, 3])), path)
                return carry

            lax.fori_loop(0, 3, one, 0)
            scatter.start(path, ring)
        if ring != 2:
            previous = order[order.index(ring) - 1]
            for path in (0, 1):
                scatter.forward(path, previous)
    for path in (0, 1):

        def own(n, carry):
            visit(place_at(path, choose(n, [2, 1, 3]), 0), path)
            return carry

        lax.fori_loop(0, 3, own, 0)
    for path in (0, 1):
        scatter.forward(path, 0)
    for ring in (2, 1, 3):
        for path in (0, 1):
            scatter.settle(path, ring)
    for path in (0, 1):
        scatter.start(path, 4)
    for b in range(buckets):
        back(place, b, True)
    for path in (0, 1):
        scatter.settle(path, 0)
        scatter.forward(path, 4)
    cosine, sine = local_angles(inner_ref, outer_ref, place)

    def turn_back(values):
        return values * cosine - turned(values) * sine

    gain_sum = jnp.zeros((1, size), f32)
    for b in range(buckets):
        rows = slice(b * block, (b + 1) * block)
        grad_rot = grad_turned[b].T * scale
        for h in range(heads):
            cols = slice(h * size, (h + 1) * size)
            unit, inverse = unit_scale(query_raw_ref[rows, cols])
            straight = turn_back(grad_rot[h * block : (h + 1) * block])
            gain_sum += jnp.sum(straight * unit, axis=0, keepdims=True)
            grad_query_out[rows, cols] = norm_back(
                straight * gain_query_ref[...], unit, inverse
            ).astype(bf16)
    gain_query_out[...] = gain_sum
    gain_sum = jnp.zeros((1, size), f32)
    spots = place * block + lax.broadcasted_iota(jnp.int32, (block, size), 0)
    for b in range(buckets):
        rows = slice(b * block, (b + 1) * block)
        live = spots < lengths_ref[b]
        grad_keys, grad_vals = scatter.total(b, 4)
        grad_value_out[rows, :] = jnp.where(live, grad_vals, 0.0).astype(bf16)
        unit, inverse = unit_scale(key_raw_ref[rows, :])
        straight = turn_back(jnp.where(live, grad_keys, 0.0))
        gain_sum += jnp.sum(straight * unit, axis=0, keepdims=True)
        grad_key_out[rows, :] = norm_back(straight * gain_key_ref[...], unit, inverse).astype(bf16)
    gain_key_out[...] = gain_sum
    scatter.finish()


def attend_back(
    call_id, lengths, grad, w_out, attended, logits, query, lse, raws, gains, tables, kv
):
    rows = grad.shape[0]
    places, buckets, _, block, size = kv.shape
    heads = w_out.shape[0] // size
    vmem = pl.BlockSpec(memory_space=pltpu.VMEM)
    shape = jax.ShapeDtypeStruct
    return pl.pallas_call(
        back_kernel,
        name="attend_back",
        out_shape=(
            shape((rows, heads * size), bf16),
            shape((rows, size), bf16),
            shape((rows, size), bf16),
            shape((rows, heads), bf16),
            shape((1, size), f32),
            shape((1, size), f32),
        ),
        in_specs=[pl.BlockSpec(memory_space=pltpu.SMEM)]
        + [vmem] * 12
        + [pl.BlockSpec(memory_space=pl.ANY)],
        out_specs=(vmem,) * 6,
        scratch_shapes=[
            pltpu.VMEM(kv.shape, bf16),
            pltpu.VMEM(kv.shape, bf16),
            pltpu.VMEM((2, 5, 6, block, size), bf16),
            pltpu.VMEM((buckets, heads * block, size), bf16),
            pltpu.VMEM((buckets, 8, heads * block), f32),
            pltpu.VMEM((buckets, 8, heads * block), f32),
            pltpu.VMEM((buckets, size, heads * block), f32),
            pltpu.SemaphoreType.DMA((2, 60)),
            pltpu.SemaphoreType.DMA((1,)),
        ],
        compiler_params=pltpu.CompilerParams(
            collective_id=call_id, has_side_effects=True, vmem_limit_bytes=VMEM_LIMIT
        ),
        cost_estimate=pl.CostEstimate(
            flops=8 * 2**30, bytes_accessed=16 * 2**20, transcendentals=2**22
        ),
    )(lengths, grad, w_out, attended, logits, query, lse, *raws, *gains, *tables, kv)


def local(
    tokens,
    lengths,
    norm_attn,
    w_query,
    w_key,
    w_value,
    w_gate,
    norm_query,
    norm_key,
    w_out,
    norm_ffn,
    w_ffn_gate,
    w_ffn_up,
    w_down,
    cotangent,
):
    buckets, per_device, model_width = tokens.shape
    head_count = w_gate.shape[1]
    head_size = norm_query.shape[0]
    kv_count = w_key.shape[1] // head_size
    group_size = head_count // kv_count
    total_rows = buckets * per_device
    full_len = per_device * lax.axis_size(SEQ)
    positions = lax.axis_index(SEQ) * per_device + jnp.arange(per_device, dtype=jnp.int32)
    share_rows = total_rows // lax.axis_size(GRP)
    share_start = lax.axis_index(GRP) * share_rows

    def take_share(values):
        return lax.dynamic_slice_in_dim(values, share_start, share_rows, 0)

    flat = tokens.reshape(total_rows, model_width)
    tables = angle_tables(per_device, head_size, lax.axis_size(SEQ))
    gains_in = (norm_query.reshape(1, -1), norm_key.reshape(1, -1))
    normed, query_raw, key_raw, logits, query_low, pairs, attended, lse, gated = attend(
        5, lengths, flat, norm_attn.reshape(1, -1), w_query, w_key, w_value, w_gate, *gains_in, tables
    )
    base = take_share(flat)
    share = jax.ShapeDtypeStruct((share_rows, model_width), f32)
    scale = jax.ShapeDtypeStruct((share_rows, 1), f32)
    gain_row = jax.ShapeDtypeStruct((1, model_width), f32)
    middle, inverse_two, normed_two = exchange_rows(
        "attention_rows",
        1,
        (gated,),
        (w_out,),
        False,
        finish_middle,
        (base, norm_ffn.reshape(1, -1)),
        (share, scale),
    )
    live_rows = (positions[None, :] < lengths[:, None]).astype(f32)
    loss_ratio = buckets * full_len / jnp.sum(lengths).astype(f32)
    grad_out = (cotangent.astype(f32) * live_rows[:, :, None] * loss_ratio).reshape(
        total_rows, model_width
    )
    grad_out_low = grad_out.astype(bf16)
    hidden, grad_gate_pre, grad_up, grad_down, grad_ffn_gate, grad_ffn_up = feed_forward(
        normed_two, grad_out_low, w_ffn_gate, w_ffn_up, w_down
    )
    ffn_sums = lax.psum((grad_ffn_gate, grad_ffn_up, grad_down), SEQ)
    grad_middle, ffn_gain_part, grad_attn_low = exchange_rows(
        "feed_back_rows",
        2,
        (grad_gate_pre, grad_up),
        (w_ffn_gate, w_ffn_up),
        True,
        finish_grad_middle,
        (middle, inverse_two, norm_ffn.reshape(1, -1), take_share(grad_out)),
        (share, gain_row),
    )
    (mixed,) = exchange_rows(
        "mixed_rows", 3, (hidden,), (w_down,), False, finish_plain, (middle,), ()
    )
    mixed = mixed.reshape(buckets, per_device, model_width)
    grad_w_out = jnp.dot(gated.T, grad_attn_low, preferred_element_type=f32)
    grad_query_low, grad_key_low, grad_value_low, grad_logits, query_gain, key_gain = attend_back(
        6,
        lengths,
        grad_attn_low,
        w_out,
        attended,
        logits,
        query_low,
        lse,
        (query_raw, key_raw),
        gains_in,
        tables,
        pairs,
    )
    grad_w_query = jnp.dot(normed.T, grad_query_low, preferred_element_type=f32)
    grad_w_key = jnp.dot(normed.T, grad_key_low, preferred_element_type=f32)
    grad_w_value = jnp.dot(normed.T, grad_value_low, preferred_element_type=f32)
    grad_w_gate = jnp.dot(normed.T, grad_logits, preferred_element_type=f32)
    attn_gain_part, grad_tokens = exchange_rows(
        "token_rows",
        4,
        (grad_query_low, grad_key_low, grad_value_low, grad_logits),
        (w_query, w_key, w_value, w_gate),
        True,
        finish_grad_tokens,
        (base, norm_attn.reshape(1, -1), grad_middle),
        (gain_row,),
    )
    grad_tokens = grad_tokens.reshape(buckets, per_device, model_width)
    gains = jnp.concatenate(
        (ffn_gain_part[0], attn_gain_part[0], query_gain[0], key_gain[0])
    )
    grad_norm_ffn, grad_norm_attn, grad_norm_query, grad_norm_key = jnp.split(
        lax.psum(gains, SEQ_GRP),
        (model_width, 2 * model_width, 2 * model_width + head_size),
    )
    attn_parts = tuple(
        part.astype(bf16)
        for part in (grad_w_query, grad_w_key, grad_w_value, grad_w_gate, grad_w_out)
    )
    attn_parts, ffn_sums = lax.optimization_barrier((attn_parts, ffn_sums))
    attn_sums = tuple(part.astype(f32) for part in lax.psum(attn_parts, SEQ))
    ffn_sums = tuple(part.astype(f32) for part in ffn_sums)
    return (
        mixed,
        grad_tokens,
        grad_norm_attn,
        attn_sums[0],
        attn_sums[1],
        attn_sums[2],
        attn_sums[3],
        grad_norm_query,
        grad_norm_key,
        attn_sums[4],
        grad_norm_ffn,
        ffn_sums[0],
        ffn_sums[1],
        ffn_sums[2],
    )


def solution(mesh):
    finer = Mesh(mesh.devices.reshape(4, 4, 4, 2), ("seq_0", "seq_1", "grp_0", "grp_1"))
    return jax.shard_map(
        local,
        mesh=finer,
        in_specs=(
            P(None, SEQ, None),
            P(),
            P(),
            P(None, GRP),
            P(None, GRP),
            P(None, GRP),
            P(None, GRP),
            P(),
            P(),
            P(GRP, None),
            P(),
            P(None, GRP),
            P(None, GRP),
            P(GRP, None),
            P(None, SEQ, None),
        ),
        out_specs=(
            P(None, SEQ, None),
            P(None, SEQ, None),
            P(),
            P(None, GRP),
            P(None, GRP),
            P(None, GRP),
            P(None, GRP),
            P(),
            P(),
            P(GRP, None),
            P(),
            P(None, GRP),
            P(None, GRP),
            P(GRP, None),
        ),
        check_vma=False,
    )
```

time: 630 us -> 461 us (0.73)
  Pallas kernels: 0 us -> 228 us
  waiting for transfers between devices: 211 us -> 71.6 us
  matrix products: 96.7 us -> 7.92 us
  other arithmetic: 81.9 us -> 23.4 us
  blocking collectives: 153 us -> 96.2 us
  starting transfers between devices: 31.4 us -> 0.26 us
  local copies, waits for them, and re-layouts: 36 us -> 12.2 us
    pallas_call x0 -> x7, Pallas kernels: none -> 228 us  [the longest x4 132 us: exchange_rows(): pl.pallas_call(body, name=name, out_shape=tuple(out_shapes) + (jax.ShapeD...]
    all_to_all x6 -> x0, waiting for transfers between devices: 111 us -> none  [the longest x3 67.8 us: sent_and_summed(): lax.all_to_all(in_blocks(value, dim, count), axis, 0, 0, tiled=True)]
    dot_general x25 -> x0, matrix products: 89.7 us -> none  [the longest x1 12.2 us: local(): jnp.einsum('bqkgd,blkd->bkgql', grad_attended, values_all, preferred_elem...]
    all_to_all x2 -> x0, blocking collectives: 63.2 us -> none  [the longest x1 33.3 us: sent_and_summed(): lax.all_to_all(in_blocks(value, dim, count), axis, 0, 0, tiled=True)]
    psum x1 -> x2, waiting for transfers between devices: 13.3 us -> 71.6 us  [the longest x1 71.6 us: local(): ffn_sums = lax.psum((grad_ffn_gate, grad_ffn_up, grad_down), SEQ)]
    reduce_scatter x1 -> x0, waiting for transfers between devices: 49.8 us -> none  [sent_together_2(): lax.psum_scatter(both, axis, scatter_dimension=dim, tiled=True)]
    all_gather x1 -> x0, waiting for transfers between devices: 37.5 us -> none  [sent_together(): lax.all_gather(both, axis, axis=dim, tiled=True)]
    all_to_all x6 -> x0, starting transfers between devices: 30.7 us -> none  [the longest x3 15.7 us: sent_to_all(): return lax.all_to_all(copies, axis, split_axis=0, concat_axis=0, tiled=True)]
  transfers between devices with their start and end apart: 9 -> 2, of which waited for: 8 -> 1; matrix products, arithmetic and copies ran while one was open for 11% -> 5% of each run, Pallas kernels for 0% -> 30%
where the time goes in v1:
time: 461 us; the launch traced here: 454 us
  Pallas kernels  228 us (49%)
  blocking collectives  96.2 us (21%)
  waiting for transfers between devices  71.6 us (16%)
  other arithmetic  23.4 us (5%)
  between operations  15 us (3%)
  local copies, waits for them, and re-layouts  12.2 us (3%)
  matrix products  7.92 us (2%)
    pallas_call x4, Pallas kernels, exchange_rows(): pl.pallas_call(body, name=name, out_shape=tuple(out_shapes) + (jax.ShapeD...  132 us
    psum x1, waiting for transfers between devices, local(): ffn_sums = lax.psum((grad_ffn_gate, grad_ffn_up, grad_down), SEQ)  71.6 us
    psum x1, blocking collectives, local(): lax.psum(gains, SEQ_GRP)  64.9 us
    pallas_call x1, Pallas kernels, attend_back(): pl.pallas_call(back_kernel, name='attend_back', out_shape=(shape((rows, h...  42 us
    pallas_call x1, Pallas kernels, attend(): pl.pallas_call(attend_kernel, name='attend', out_shape=(shape((rows, widt...  37.5 us
    psum x1, blocking collectives, local(): attn_sums = tuple((part.astype(f32) for part in lax.psum(attn_parts, SEQ)))  31.3 us
    pallas_call x1, Pallas kernels, feed_forward(): pl.pallas_call(feed_kernel, name='feed_forward', grid=(units // step,), i...  16.4 us
    convert_element_type x3, other arithmetic, local(): ffn_sums = tuple((part.astype(f32) for part in ffn_sums))  9.93 us
  transfers between devices with their start and end apart: 2, of which 1 were waited for; matrix products, arithmetic and copies ran while one was open for 5% of the time, Pallas kernels for 30%

profile of v1, /device:TPU:1, one launch (start us, length us, event | category | flops | bytes accessed | tf_op | source)
XLA Modules:
  0.0 454.1 jit_solution(16077705849067914920)
XLA Ops:
  9.9 1.8 copy.31.w_gate_ref.refs_7_
  11.7 2.1 multiply_multiply_fusion
  13.8 2.0 copy-done.1
  15.8 1.6 bitcast_convert_fusion.seed_ref
  17.4 1.7 constant_dynamic-slice_fusion.1.refs_2_.refs_8_
  19.1 37.5 %attend.1 = (bf16[512,2048]{1,0:T(8,128)(2,1)}, f32[512,256]{1,0:T(8,128)}, f32[512,128]{1,0:T(8,128)}, f32[512,2]{1,0:T(8,128)}, bf16[2,512,128]{2,1,0:T(8,128)...) custom-call(s32[2]{0:T(128)} %lengths_ref.3, ...), custom_call_target="tpu_custom_call" | custom-call | flops 4294967296 | bytes 16777216 | tf_op jit(solution)/shard_map/attend/pallas_call | solution.py:697
  56.6 35.5 %attention_rows.1 = (f32[64,2048]{1,0:T(8,128)}, f32[64,1]{1,0:T(8,128)}, bf16[512,2048]{1,0:T(8,128)(2,1)}) custom-call(bf16[512,256]{1,0:T(8,128)(2,1)} %get-tuple-element.51.refs_0_, bf16[256,2048]{1,0:T(8,128)(2,1)} %w_out_ref.1, bf16[64,2048]{1,0:T(8,128)(2,1)} %constant_dynamic-slice_fusion.1.refs_2_.refs_8_, f32[1,2048]{1,0:T(1,128)} %bitcast.34), custom_call_target="tpu_custom_call" | custom-call | flops 536870912 | bytes 16777216 | tf_op jit(solution)/shard_map/attention_rows/pallas_call | solution.py:235
  92.1 16.4 %feed_forward.1 = (bf16[512,768]{1,0:T(8,128)(2,1)}, bf16[512,768]{1,0:T(8,128)(2,1)}, bf16[512,768]{1,0:T(8,128)(2,1)}, bf16[768,2048]{1,0:T(8,128)(2,1)}, bf16...) custom-call(bf16[512,2048]{1,0:T(8,128)(2,1)} %get-tuple-element.52.rows_ref, ...), custom_call_target="tpu_custom_call" | custom-call | flops 9663676416 | bytes 25165824 | tf_op jit(solution)/shard_map/feed_forward/pallas_call | solution.py:332
  108.7 1.9 constant_dynamic-slice_fusion.refs_7_
  110.6 33.2 %feed_back_rows.1 = (f32[64,2048]{1,0:T(8,128)}, f32[1,2048]{1,0:T(1,128)}, bf16[512,2048]{1,0:T(8,128)(2,1)}) custom-call(bf16[512,768]{1,0:T(8,128)(2,1)} %get-tuple-element.55.refs_0_, bf16[512,768]{1,0:T(8,128)(2,1)} %get-tuple-element.56.refs_1_, bf16[2048,768]{1,0:T(8,128)(2,1)} %refs_2_.1, bf16[2048,768]{1,0:T(8,128)(2,1)} %refs_3_.1, ...), custom_call_target="tpu_custom_call" | custom-call | flops 3221225472 | bytes 16777216 | tf_op jit(solution)/shard_map/feed_back_rows/pallas_call | solution.py:235
  143.8 42.0 %attend_back.1 = (bf16[512,256]{1,0:T(8,128)(2,1)}, bf16[512,128]{1,0:T(8,128)(2,1)}, bf16[512,128]{1,0:T(8,128)(2,1)}, bf16[512,2]{1,0:T(8,128)(2,1)}, f32[1,128]{1,0:T(1,128)}, /*index=5*/f32[1,128]{1,0:T(1,128)}) custom-call(s32[2]{0:T(128)} %lengths_ref.3, bf16[512,2048]{1,0:T(8,128)(2,1)} %get-tuple-element.58.grad_ref, bf16[256,2048]{1,0:T(8,128)(2,1)} %w_out_ref.1, ...), custom_call_target="tpu_custom_call" | custom-call | flops 8589934592 | bytes 16777216 | tf_op jit(solution)/shard_map/attend_back/pallas_call | solution.py:897
  187.2 1.6 convolution_convert_fusion.3
  188.8 1.6 convolution_convert_fusion.2
  190.4 1.7 convolution_convert_fusion
  192.1 1.7 convolution_convert_fusion.1
  193.8 71.6 %all-reduce.7.cloned.1.call-done = (bf16[2048,768]{1,0:T(8,128)(2,1)}, bf16[2048,768]{1,0:T(8,128)(2,1)}, bf16[768,2048]{1,0:T(8,128)(2,1)}) async-done(((bf16[2048,768]{1,0:T(8,128)(2,1)}, bf16[2048,768]{1,0:T(8,128)(2,1)}, bf16[768,2048]{1,0:T(8,128)(2,1)}), (bf16[2048,768]{1,0:T(8,128)(2,1)}, bf16[2048,768]{1,0:T(8,128)(2,1)}, bf16[768,2048]{1,0:T(8,128)(2,1)})) %all-reduce.7.cloned.1.call-update) | async-done | bytes 9437200 | tf_op jit(solution)/shard_map/psum | solution.py:992
  265.4 32.9 %mixed_rows.1 = bf16[512,2048]{1,0:T(8,128)(2,1)} custom-call(bf16[512,768]{1,0:T(8,128)(2,1)} %get-tuple-element.53.refs_0_, bf16[768,2048]{1,0:T(8,128)(2,1)} %refs_1_.3, f32[64,2048]{1,0:T(8,128)} %get-tuple-element.54.refs_2_.refs_4_), custom_call_target="tpu_custom_call" | custom-call | flops 1610612736 | bytes 16777216 | tf_op jit(solution)/shard_map/mixed_rows/pallas_call | solution.py:235
  298.4 30.2 %token_rows.1 = (f32[1,2048]{1,0:T(1,128)}, bf16[512,2048]{1,0:T(8,128)(2,1)}) custom-call(bf16[512,256]{1,0:T(8,128)(2,1)} %get-tuple-element.66.refs_0_, bf16[512,128]{1,0:T(8,128)(2,1)} %get-tuple-element.67.refs_1_, bf16[512,128]{1,0:T(8,128)(2,1)} %get-tuple-element.68.refs_2_, bf16[512,2]{1,0:T(8,128)(2,1)} %get-tuple-element.69.refs_3_, ...), custom_call_target="tpu_custom_call" | custom-call | flops 1077936128 | bytes 16777216 | tf_op jit(solution)/shard_map/token_rows/pallas_call | solution.py:235
  329.3 64.9 %psum.63 = f32[4352]{0:T(1024)S(1)} all-reduce(f32[4352]{0:T(1024)S(1)} %pad_maximum_fusion), channel_id=1, replica_groups=mesh['seq_0'=4,'seq_1'=4,'grp_0'=4,'grp_1'=2] {'seq_0','seq_1','grp_0','..., use_global_device_ids=true, to_apply=%region_1.0 | all-reduce | flops 4352 | bytes 34816 | tf_op jit(solution)/shard_map/psum | solution.py:1041
  395.3 31.3 %psum.70 = bf16[2048,2]{0,1:T(2,128)(2,1)S(1)} all-reduce(bf16[2048,2]{0,1:T(2,128)(2,1)S(1)} %convolution_convert_fusion.4), channel_id=1, replica_groups=mesh['seq_0'=4,'seq_1'=4,'grp_0'=4,'grp_1'=2] {'seq_0','seq_1'}, use_global_device_ids=true, to_apply=%region_8.0 | all-reduce | flops 4096 | bytes 16384 | tf_op jit(solution)/shard_map/psum | solution.py:1049
  427.3 3.2 convert_element_type.69
  430.4 3.2 convert_element_type.70
  433.6 3.6 convert_element_type.71
  437.2 2.8 convert_element_type.64
  (53 shorter events, 13.6 us)
Async XLA Ops:
  7.2 258.2 %all-reduce.7.cloned.1.call-start = ((), (), s32[]{:S(2)}) async-start(), calls=%async_computation.1 | async-start | bytes 18874368 | tf_op jit(solution)/shard_map/psum | solution.py:992
  13.8 2.0 copy-start.1
  108.5 328.7 %all-reduce.5.cloned.1.call-start = ((), (), s32[]{:S(2)}) async-start(), calls=%async_computation | async-start | bytes 6291456 | tf_op jit(solution)/shard_map/psum | solution.py:1049
  143.8 42.0 %copy-start = (bf16[512,2048]{1,0:T(8,128)(2,1)S(1)}, bf16[512,2048]{1,0:T(8,128)(2,1)}, u32[]{:S(2)}) copy-start(bf16[512,2048]{1,0:T(8,128)(2,1)} %get-tuple-element.76) | copy-start | bytes 6291460
  185.8 1.4 copy-start.11
  187.2 1.6 copy-start.12
  188.8 1.6 copy-start.7
  188.8 1.6 copy-start.14
  190.4 1.7 copy-start.13
  298.3 30.2 %copy-start.15 = (f32[1,2048]{1,0:T(1,128)S(1)}, f32[1,2048]{1,0:T(1,128)}, u32[]{:S(2)}) copy-start(f32[1,2048]{1,0:T(1,128)} %get-tuple-element.72) | copy-start | bytes 24580
  298.3 30.2 %copy-start.16 = (f32[1,128]{1,0:T(1,128)S(1)}, f32[1,128]{1,0:T(1,128)}, u32[]{:S(2)}) copy-start(f32[1,128]{1,0:T(1,128)} %get-tuple-element.74) | copy-start | bytes 1540
  298.3 30.2 %copy-start.17 = (f32[1,128]{1,0:T(1,128)S(1)}, f32[1,128]{1,0:T(1,128)}, u32[]{:S(2)}) copy-start(f32[1,128]{1,0:T(1,128)} %get-tuple-element.75) | copy-start | bytes 1540
  298.4 128.9 %copy-start.5 = (bf16[2048,768]{1,0:T(8,128)(2,1)S(1)}, bf16[2048,768]{1,0:T(8,128)(2,1)}, u32[]{:S(2)}) copy-start(bf16[2048,768]{1,0:T(8,128)(2,1)} %get-tuple-element.85) | copy-start | bytes 9437188
  427.3 3.2 copy-start.4
  430.4 3.2 copy-start.3
  437.2 2.8 copy-start.10
  437.2 3.8 copy-start.9
  440.0 2.1 copy-start.8
  441.0 2.6 copy-start.2
  443.6 2.3 copy-start.6
Sparse Core Ops, SparseCore 0:
  108.6 156.7 all-reduce.6
  270.7 95.3 all-reduce.4
